TPU v7x, 512 devices: a whole 4x4x16 slice. The times are simulated.
512 devices in a mesh: queue: 16 (over x, y_hi, core), seq: 32 (over z, y_lo).
Axes of the slice: x: 4, y: 4 (y_hi: 2, y_lo: 2; y = y_hi * 2 + y_lo), z: 16, core: 2. Of those that a mesh axis runs over, the one named last changes fastest.
Arguments:
- projected: bfloat16 [3, 24576, 4096], P(None, ('queue', 'seq')), may hold values from -8 to 8
- out_weight: bfloat16 [5120, 4096], P('seq'), may hold values from -2 to 2
- head_weight: bfloat16 [5120, 64], P('seq'), may hold values from -0.078125 to 0.078125
- hidden_in: bfloat16 [5120, 24576], P('seq', 'queue'), may hold values from -30 to 30
- latent: float32 [24576, 64], P(('queue', 'seq')), may hold values from -6 to 6
- fresh_noise: float32 [1536, 64], P('seq'), may hold values from -6 to 6
- levels: int32 [16], P('queue'), may hold values from 0 to 49
Outputs:
- block_out: float32 [5120, 24576], P('seq', 'queue')
- velocity: float32 [24576, 64], P(('queue', 'seq'))
- queue_next: float32 [24576, 64], P(('queue', 'seq'))
All inputs are finite; a program needn't handle non-finite values.
Results may differ from a plain program's by a relative error of at most 0.0042.
Values may be sent and summed in bfloat16 or wider, within the bound.
A program may use at most 64 MiB of HBM per device.

v0:
```python
import math

import jax
import jax.numpy as jnp
from jax import lax
from jax.sharding import PartitionSpec as P

DOUT = 5120
H = 32
HD = 128
STEPS = 50


def from_behind(block, axis, distance):
    devices = range(lax.axis_size(axis))
    route = [(i - distance, i) for i in devices if i - distance in devices]
    return lax.ppermute(block, axis, route)


def attend(queries, keys, values):
    length = queries.shape[0]
    block = math.gcd(length, 512)
    grouped = queries.reshape(length // block, block, queries.shape[1])

    def one_block(query_block):
        scores = lax.dot_general(
            query_block, keys, (((1,), (1,)), ((), ())), preferred_element_type=jnp.float32
        )
        scores = scores * queries.shape[1] ** (-0.5)
        peak = jnp.max(scores, axis=1, keepdims=True)
        raw = jnp.exp(scores - peak)
        total = jnp.sum(raw, axis=1, keepdims=True)
        probs = raw.astype(jnp.bfloat16)
        mixed = jnp.dot(probs, values, preferred_element_type=jnp.float32) / total
        return mixed.astype(jnp.bfloat16)

    return lax.map(one_block, grouped).reshape(length, queries.shape[1])


def sigma_of(level):
    frac = 1.0 - level / STEPS
    return 5.0 * frac / (1.0 + 4.0 * frac)


def contract_last(weight, rows):
    return lax.dot_general(
        weight, rows, (((1,), (1,)), ((), ())), preferred_element_type=jnp.float32
    )


def on_device(projected, out_weight, head_weight, hidden_in, latent, fresh_noise, levels):
    heads_here = H // lax.axis_size("seq")
    by_head = lax.all_to_all(projected, "seq", split_axis=2, concat_axis=1, tiled=True)
    seq_len = by_head.shape[1]
    head_view = by_head.reshape(3, seq_len, heads_here, HD)
    results = attend(head_view[0, :, 0], head_view[1, :, 0], head_view[2, :, 0])
    update = contract_last(out_weight, lax.all_gather(results, "seq", axis=1, tiled=True))
    block_out = hidden_in.astype(jnp.float32) + update
    squares = lax.psum(jnp.sum(block_out * block_out, axis=0), "seq")
    scale = lax.rsqrt(squares / DOUT + 1e-06)
    normed = (block_out * scale[None, :]).astype(jnp.bfloat16)
    velocity = lax.psum_scatter(
        lax.dot_general(
            normed, head_weight, (((0,), (0,)), ((), ())), preferred_element_type=jnp.float32
        ),
        "seq",
        scatter_dimension=0,
        tiled=True,
    )
    level_now = levels[0].astype(jnp.float32)
    delta = sigma_of(level_now + 1.0) - sigma_of(level_now)
    stepped = latent + delta * velocity
    shifted = from_behind(stepped, "queue", 1)
    queue_next = jnp.where(lax.axis_index("queue") == 0, fresh_noise, shifted)
    return (block_out, velocity, queue_next)


def solution(mesh):
    placed = (
        P(None, ("queue", "seq"), None),
        P("seq", None),
        P("seq", None),
        P("seq", "queue"),
        P(("queue", "seq"), None),
        P("seq", None),
        P("queue"),
    )
    return jax.shard_map(
        on_device,
        mesh=mesh,
        in_specs=placed,
        out_specs=(P("seq", "queue"), P(("queue", "seq"), None), P(("queue", "seq"), None)),
        check_vma=False,
    )
```

profile of v0, /device:TPU:1, one launch (start us, length us, event | category | flops | bytes accessed | tf_op | source)
XLA Modules:
  0.0 681.2 jit_solution(17592238812296847051)
XLA Ops:
  7.2 0.0 copy-start
  7.2 6.3 copy.11
  13.5 8.1 %reshape.47 = bf16[32,2,9216]{2,1,0:T(2,128)(2,1)} reshape(bf16[4096,3,48]{2,1,0:T(4,128)(2,1)} %bitcast.37) | data formatting | bytes 2359296
  21.5 17.0 %all-to-all-start = ((bf16[32,2,9216]{2,1,0:T(2,128)(2,1)}), bf16[32,2,9216]{2,1,0:T(2,128)(2,1)S(1)}, u32[]{:S(2)}, u32[]{:S(2)}) async-start(bf16[32,2,9216]{2,1,0:T(2,128)(2,1)} %reshape.47), calls=%async_computation | async-start | bytes 2359296 | tf_op jit(solution)/shard_map/all_to_all | solution.py:53
  38.6 0.0 all-gather.2.cloned.1.call-start
  38.6 58.4 %all-to-all-done = bf16[32,2,9216]{2,1,0:T(2,128)(2,1)S(1)} async-done(((bf16[32,2,9216]{2,1,0:T(2,128)(2,1)}), bf16[32,2,9216]{2,1,0:T(2,128)(2,1)S(1)}, u32[]{:S(2)}, u32[]{:S(2)}) %all-to-all-start) | async-done | bytes 1179680 | tf_op jit(solution)/shard_map/all_to_all | solution.py:53
  97.1 6.6 reshape.48
  103.7 12.1 %fusion.24 = (bf16[1,32,48,128]{2,0,3,1:T(2,128)(2,1)}, bf16[1,32,48,128]{2,0,3,1:T(2,128)(2,1)}, bf16[1,32,48,128]{2,0,3,1:T(2,128)(2,1)S(1)}) fusion(bf16[3,32,48,128]{2,0,3,1:T(4,128)(2,1)} %bitcast.36), kind=kLoop, calls=%fused_computation.23 | loop fusion | bytes 2359296 | tf_op jit(solution)/shard_map/slice | solution.py:56
  115.8 3.5 copy.12
  119.3 0.0 copy-start.2
  119.3 4.6 copy.13
  123.9 4.6 copy.14
  128.5 0.0 copy-done.2
  128.5 0.0 copy-start.7
  128.5 8.6 %while.10 = (s32[]{:T(128)}, bf16[3,512,128]{2,1,0:T(8,128)(2,1)S(1)}, bf16[3,512,128]{2,1,0:T(8,128)(2,1)}, bf16[1536,128]{1,0:T(8,128)(2,1)S(1)}, bf16[1536,128]{1,0:T(8,128)(2,1)S(1)}, /*index=5*/s32[]{:T(128)}) while((s32[]{:T(128)}, bf16[3,512,128]{2,1,0:T(8,128)(2,1)S(1)}, bf16[3,512,128]{2,1,0:T(8,128)(2,1)}, ...), condition=%wide.region_3.4_spmd, body=%wide.region_0.3_spmd.sunk | while | flops 407501824 | bytes 10496585 | solution.py:37
  128.6 1.6 fusion.39
  130.2 0.6 fusion.40
  130.7 0.7 fusion.41
  131.5 1.6 fusion.39
  133.0 0.6 fusion.40
  133.6 0.7 fusion.41
  134.3 1.6 fusion.39
  135.9 0.6 fusion.40
  136.5 0.7 fusion.41
  137.2 0.0 copy-start.3
  137.2 0.7 copy-done.3
  137.9 0.0 all-gather.2.cloned.1.call-update
  138.0 0.0 copy-start.4
  138.0 0.0 copy-start.5
  138.0 0.0 copy-start.6
  138.0 0.0 reduce-scatter.2.cloned.1.call-start
  138.0 304.1 %all-gather.2.cloned.1.call-done = bf16[1536,4096]{1,0:T(8,128)(2,1)} async-done(((bf16[1536,128]{1,0:T(8,128)(2,1)}), bf16[1536,4096]{1,0:T(8,128)(2,1)}) %all-gather.2.cloned.1.call-update) | async-done | bytes 12582928 | tf_op jit(solution)/shard_map/all_gather | solution.py:57
  442.2 0.0 copy-done
  442.2 0.0 copy-done.7
  442.2 8.9 %multiply_reduce_fusion = (f32[1536]{0:T(1024)S(1)}, f32[160,1536]{1,0:T(8,128)S(1)}) fusion(bf16[1536,4096]{1,0:T(8,128)(2,1)} %all-gather.2.cloned.1.call-done, bf16[160,4096]{1,0:T(8,128)(2,1)S(1)} %copy-done, bf16[160,1536]{1,0:T(8,128)(2,1)S(1)} %copy-done.7), kind=kOutput, calls=%fused_computation.16 | convolution fusion | flops 2014247424 | bytes 15374336 | tf_op jit(solution)/shard_map/dot_general | solution.py:46
  451.1 0.0 copy-start.1
  451.1 49.7 %psum.7 = f32[1536]{0:T(1024)S(1)} all-reduce(f32[1536]{0:T(1024)S(1)} %get-tuple-element.46), channel_id=1, replica_groups=mesh['queue'=16,'seq'=32] {'seq'}, use_global_device_ids=true, to_apply=%region_5.6 | all-reduce | flops 1536 | bytes 12288 | tf_op jit(solution)/shard_map/psum | solution.py:59
  500.7 0.0 copy-done.4
  500.8 1.3 fusion.21
  502.1 0.0 reduce-scatter.2.cloned.1.call-update
  502.8 140.0 %reduce-scatter.2.cloned.1.call-done = f32[48,64]{1,0:T(8,128)} async-done(((f32[1536,64]{1,0:T(8,128)}), f32[48,64]{1,0:T(8,128)}) %reduce-scatter.2.cloned.1.call-update) | async-done | bytes 12304 | tf_op jit(solution)/shard_map/reduce_scatter | solution.py:62
  642.9 0.0 copy-done.5
  642.9 0.7 multiply_add_fusion
  643.6 29.2 %collective-permute-start = (f32[48,64]{1,0:T(8,128)S(1)}, f32[48,64]{1,0:T(8,128)S(1)}, u32[]{:S(2)}, u32[]{:S(2)}) collective-permute-start(f32[48,64]{1,0:T(8,128)S(1)} %multiply_add_fusion), channel_id=1, source_target_pairs={{0,32},{32,64},{64,96},{96,128},{128,160},{160,192},{192,224},{224... | collective-permute-start | bytes 36872 | tf_op jit(solution)/shard_map/ppermute | solution.py:17
  672.8 0.9 collective-permute-done
  673.7 0.0 copy-done.6
  673.7 0.6 broadcast_select_fusion
  674.4 0.0 copy-done.1
  (2 shorter events, 0.0 us)
Async XLA Ops:
  7.2 435.0 %copy-start = (bf16[160,4096]{1,0:T(8,128)(2,1)S(1)}, bf16[160,4096]{1,0:T(8,128)(2,1)}, u32[]{:S(2)}) copy-start(bf16[160,4096]{1,0:T(8,128)(2,1)} %param.10) | copy-start | bytes 3932164
  21.5 75.5 %all-to-all-start = ((bf16[32,2,9216]{2,1,0:T(2,128)(2,1)}), bf16[32,2,9216]{2,1,0:T(2,128)(2,1)S(1)}, u32[]{:S(2)}, u32[]{:S(2)}) async-start(bf16[32,2,9216]{2,1,0:T(2,128)(2,1)} %reshape.47), calls=%async_computation | async-start | bytes 2359296 | tf_op jit(solution)/shard_map/all_to_all | solution.py:53
  38.6 403.6 %all-gather.2.cloned.1.call-start = ((), (), s32[]{:S(2)}) async-start(), calls=%async_computation.2 | async-start | bytes 12976128 | tf_op jit(solution)/shard_map/all_gather | solution.py:57
  119.3 9.2 %copy-start.2 = (bf16[3,512,128]{2,1,0:T(8,128)(2,1)S(1)}, bf16[3,512,128]{2,1,0:T(8,128)(2,1)}, u32[]{:S(2)}) copy-start(bf16[3,512,128]{2,1,0:T(8,128)(2,1)} %custom-call) | copy-start | bytes 1179652
  128.5 313.6 %copy-start.7 = (bf16[160,1536]{1,0:T(8,128)(2,1)S(1)}, bf16[160,1536]{1,0:T(8,128)(2,1)}, u32[]{:S(2)}) copy-start(bf16[160,1536]{1,0:T(8,128)(2,1)} %param.12) | copy-start | bytes 1474564
  137.2 0.7 copy-start.3
  138.0 362.8 %copy-start.4 = (bf16[160,64]{0,1:T(8,128)(2,1)S(1)}, bf16[160,64]{0,1:T(8,128)(2,1)}, u32[]{:S(2)}) copy-start(bf16[160,64]{0,1:T(8,128)(2,1)} %param.11) | copy-start | bytes 61444
  138.0 504.9 %copy-start.5 = (f32[48,64]{1,0:T(8,128)S(1)}, f32[48,64]{1,0:T(8,128)}, u32[]{:S(2)}) copy-start(f32[48,64]{1,0:T(8,128)} %param.13) | copy-start | bytes 36868
  138.0 535.8 %copy-start.6 = (f32[48,64]{1,0:T(8,128)S(1)}, f32[48,64]{1,0:T(8,128)}, u32[]{:S(2)}) copy-start(f32[48,64]{1,0:T(8,128)} %param.14) | copy-start | bytes 36868
  138.0 504.9 %reduce-scatter.2.cloned.1.call-start = ((), (), s32[]{:S(2)}) async-start(), calls=%async_computation.3 | async-start | bytes 811008 | tf_op jit(solution)/shard_map/reduce_scatter | solution.py:62
  451.1 223.3 %copy-start.1 = (f32[160,1536]{1,0:T(8,128)}, f32[160,1536]{1,0:T(8,128)S(1)}, u32[]{:S(2)}) copy-start(f32[160,1536]{1,0:T(8,128)S(1)} %get-tuple-element.47) | copy-start | bytes 2949124
  643.6 30.1 %collective-permute-start = (f32[48,64]{1,0:T(8,128)S(1)}, f32[48,64]{1,0:T(8,128)S(1)}, u32[]{:S(2)}, u32[]{:S(2)}) collective-permute-start(f32[48,64]{1,0:T(8,128)S(1)} %multiply_add_fusion), channel_id=1, source_target_pairs={{0,32},{32,64},{64,96},{96,128},{128,160},{160,192},{192,224},{224... | collective-permute-start | bytes 36872 | tf_op jit(solution)/shard_map/ppermute | solution.py:17
Sparse Core Ops, SparseCore 0:
  138.1 304.0 all-gather.1
  502.2 140.5 reduce-scatter.1
where the time goes:
time: 683 us; the launch traced here: 681 us
  waiting for transfers between devices  504 us (74%)
  blocking collectives  49.7 us (7%)
  local copies, waits for them, and re-layouts  46.6 us (7%)
  starting transfers between devices  46.3 us (7%)
  matrix products  17.1 us (3%)
  between operations  14.9 us (2%)
    all_gather x1, waiting for transfers between devices, on_device(): lax.all_gather(results, 'seq', axis=1, tiled=True)  304 us
    reduce_scatter x1, waiting for transfers between devices, on_device(): lax.psum_scatter(lax.dot_general(normed, head_weight, (((0,), (0,)), ((),...  140 us
    all_to_all x1, waiting for transfers between devices, on_device(): lax.all_to_all(projected, 'seq', split_axis=2, concat_axis=1, tiled=True)  58.4 us
    psum x1, blocking collectives, on_device(): squares = lax.psum(jnp.sum(block_out * block_out, axis=0), 'seq')  49.7 us
    ppermute x1, starting transfers between devices, from_behind(): return lax.ppermute(block, axis, route)  29.2 us
    slice x4, local copies, waits for them, and re-layouts, on_device(): results = attend(head_view[0, :, 0], head_view[1, :, 0], head_view[2, :, 0])  24.8 us
    unnamed x19, local copies, waits for them, and re-layouts  21.7 us
    all_to_all x1, starting transfers between devices, on_device(): lax.all_to_all(projected, 'seq', split_axis=2, concat_axis=1, tiled=True)  17 us
  transfers between devices with their start and end apart: 4, of which 4 were waited for; matrix products, arithmetic and copies ran while one was open for 0% of the time, Pallas kernels for 0%

commit v1 on v0

v1 whole, which is shorter than its diff:
```python
import functools
import math

import jax
import jax.numpy as jnp
from jax import lax
from jax.experimental import pallas as pl
from jax.experimental.pallas import tpu as pltpu
from jax.sharding import PartitionSpec as P

MESH = pl.DeviceIdType.MESH
F32 = jnp.float32
BF16 = jnp.bfloat16
STEPS = 50
SKEW = 2
LOG2E = 1.4426950408889634


def contract_last(a, b):
    return lax.dot_general(a, b, (((1,), (1,)), ((), ())), preferred_element_type=F32)


def sigma_of(level):
    frac = 1.0 - level / STEPS
    return 5.0 * frac / (1.0 + 4.0 * frac)


def split_squares(vel, squares):
    lane = lax.broadcasted_iota(jnp.int32, vel.shape, 1)
    high = squares.astype(BF16).astype(F32)
    rest = squares - high
    middle = rest.astype(BF16).astype(F32)
    low = rest - middle
    tail = jnp.where(lane == 64, high, jnp.where(lane == 65, middle, jnp.where(lane == 66, low, 0.0)))
    return jnp.where(lane < 64, vel, tail).astype(BF16)


def sum_squares_lanes(total):
    lane = lax.broadcasted_iota(jnp.int32, total.shape, 1)
    return jnp.sum(jnp.where(lane >= 64, total, 0.0), axis=1, keepdims=True)


def kernel(
    n_queue, n_z, n_chunks, d_out,
    proj_hbm, w_hbm, hw_ref, hid_ref, lat_ref, fresh_ref, lev_ref,
    out_ref, vel_ref, next_ref,
    projv, qkv, vt, scores, att, wbuf, acc, hwp, rs_send, rs_recv, pay, y_recv, z_send, z_recv, n_send, n_recv,
    proj_sem, own_sem, kv_send, kv_recv, q_send, q_recv, w_own, w_send, w_recv,
    ag_send, ag_recv, rs_ssem, rs_rsem, y_ssem, y_rsem, z_ssem, z_rsem, n_ssem, n_rsem,
):
    n_seq = 2 * n_z
    half = n_z // 2
    tok = proj_hbm.shape[1]
    hd = qkv.shape[2]
    n_tok = qkv.shape[1]
    chunk = n_tok // n_chunks
    own_z = n_z // n_chunks
    rows = w_hbm.shape[0]
    group = lax.axis_index("queue")
    me = lax.axis_index("seq")
    z = me // 2
    y = me % 2
    partner = 2 * z + (1 - y)
    after = (group + 1) % n_queue
    before = (group + n_queue - 1) % n_queue

    load = pltpu.make_async_copy(proj_hbm, projv, proj_sem)
    load.start()

    @pl.loop(0, n_z)
    def _(i):
        pltpu.make_async_copy(
            w_hbm.at[:, pl.ds(pl.multiple_of((2 * i + y) * hd, hd), hd)], wbuf.at[i, pl.ds(0, rows)], w_own
        ).start()

    barrier = pltpu.get_barrier_semaphore()

    @pl.loop(1, n_seq)
    def _(i):
        pl.semaphore_signal(barrier, inc=1, device_id=(group, (me + i) % n_seq), device_id_type=MESH)

    pl.semaphore_signal(barrier, inc=1, device_id=(after, me), device_id_type=MESH)
    pl.semaphore_signal(barrier, inc=1, device_id=(before, me), device_id_type=MESH)
    hwp[...] = jnp.zeros_like(hwp)
    hwp[:, 0:64] = hw_ref[...]
    pl.semaphore_wait(barrier, n_seq + 1)
    load.wait()

    def exchange(first, count, send_sem, recv_sem):
        def to(dest):
            pltpu.make_async_remote_copy(
                src_ref=projv.at[pl.ds(first, count), :, pl.ds(pl.multiple_of(dest * hd, hd), hd)],
                dst_ref=qkv.at[pl.ds(first, count), pl.ds(pl.multiple_of(me * tok, tok), tok), :],
                send_sem=send_sem,
                recv_sem=recv_sem,
                device_id=(group, dest),
                device_id_type=MESH,
            ).start()

        to(partner)

        @pl.loop(1, n_z)
        def _(i):
            far = (i + 1) // 2
            shift = (i % 2) * far + (1 - i % 2) * (n_z - far)
            there = (z + shift) % n_z
            to(2 * there + y)
            to(2 * there + (1 - y))

    exchange(1, 2, kv_send, kv_recv)
    exchange(0, 1, q_send, q_recv)
    own = pltpu.make_async_copy(
        projv.at[:, :, pl.ds(pl.multiple_of(me * hd, hd), hd)],
        qkv.at[:, pl.ds(pl.multiple_of(me * tok, tok), tok), :],
        own_sem,
    )
    own.start()

    @pl.loop(0, n_z)
    def _(i):
        pltpu.make_async_remote_copy(
            src_ref=w_hbm.at[:, pl.ds(pl.multiple_of((2 * i + 1 - y) * hd, hd), hd)],
            dst_ref=wbuf.at[i, pl.ds(rows, rows)],
            send_sem=w_send,
            recv_sem=w_recv,
            device_id=(group, partner),
            device_id_type=MESH,
        ).start()

    def whole(ref, sem):
        return pltpu.make_async_copy(ref, ref, sem)

    others = (n_seq - 1) * tok
    own.wait()
    whole(qkv.at[pl.ds(1, 2), pl.ds(0, others)], kv_recv).wait()
    vt[...] = qkv[2].T
    whole(qkv.at[pl.ds(0, 1), pl.ds(0, others)], q_recv).wait()
    whole(wbuf.at[:, pl.ds(0, rows)], w_own).wait()
    whole(wbuf.at[:, pl.ds(rows, rows)], w_recv).wait()

    def ring(c, step, way):
        origin = (z + n_z - (step - 1)) % n_z if way == 0 else (z + step - 1) % n_z
        there = (z + 1) % n_z if way == 0 else (z + n_z - 1) % n_z

        def made(block):
            return pltpu.make_async_remote_copy(
                src_ref=block,
                dst_ref=block,
                send_sem=ag_send.at[way, c, step],
                recv_sem=ag_recv.at[way, c, step],
                device_id=(group, 2 * there + y),
                device_id_type=MESH,
            )

        return made, origin

    def ring_full(c, step, way):
        made, origin = ring(c, step, way)
        return made(att.at[origin, c])

    def ring_half(c, step, way):
        made, origin = ring(c, step, way)
        return made(att.at[origin, c, pl.ds(way * (hd // 2), hd // 2)])

    key_block = math.gcd(256, n_tok)

    def attend(c):
        queries = qkv[0, pl.ds(pl.multiple_of(c * chunk, 16), chunk), :]
        peak = jnp.full((8, chunk), -jnp.inf, F32)
        for k in range(0, n_tok, key_block):
            part = contract_last(qkv[1, k : k + key_block, :], queries)
            scores[k : k + key_block, :] = part
            peak = jnp.maximum(peak, jnp.max(part.reshape(key_block // 8, 8, chunk), axis=0))
        peak = jnp.max(peak, axis=0, keepdims=True)
        total = jnp.zeros((8, chunk), F32)
        mixed = jnp.zeros((hd, chunk), F32)
        factor = LOG2E * hd ** (-0.5)
        for k in range(0, n_tok, key_block):
            raw = jnp.exp2((scores[k : k + key_block, :] - peak) * factor)
            total = total + jnp.sum(raw.reshape(key_block // 8, 8, chunk), axis=0)
            mixed = mixed + jnp.dot(vt[:, k : k + key_block], raw.astype(BF16), preferred_element_type=F32)
        total = jnp.sum(total, axis=0, keepdims=True)
        att[z, c] = (mixed / total).astype(BF16)

    def rs_copy(c):
        return pltpu.make_async_remote_copy(
            src_ref=rs_send.at[c],
            dst_ref=rs_recv.at[c],
            send_sem=rs_ssem.at[c],
            recv_sem=rs_rsem.at[c],
            device_id=(group, partner),
            device_id_type=MESH,
        )

    def y_copy(c):
        return pltpu.make_async_remote_copy(
            src_ref=pay.at[c, 1 - y],
            dst_ref=y_recv.at[c],
            send_sem=y_ssem.at[c],
            recv_sem=y_rsem.at[c],
            device_id=(group, partner),
            device_id_type=MESH,
        )

    def z_copy(c, i):
        return pltpu.make_async_remote_copy(
            src_ref=z_send.at[c, i],
            dst_ref=z_recv.at[z],
            send_sem=z_ssem.at[c, i],
            recv_sem=z_rsem,
            device_id=(group, 2 * (c * own_z + i) + y),
            device_id_type=MESH,
        )

    def finish_block(c):
        rs_copy(c).wait_recv()
        columns = pl.ds(pl.multiple_of(c * chunk, chunk), chunk)
        x = hid_ref[:, columns].astype(F32) + acc[c, 0:rows] + rs_recv[c].astype(F32)
        out_ref[:, columns] = x
        turned = x.T
        squares = jnp.sum(turned * turned, axis=1, keepdims=True)
        upper = turned.astype(BF16)
        lower = (turned - upper.astype(F32)).astype(BF16)
        vel = jnp.dot(upper, hwp[...], preferred_element_type=F32) + jnp.dot(lower, hwp[...], preferred_element_type=F32)
        lane = lax.broadcasted_iota(jnp.int32, vel.shape, 1)
        payload = jnp.where(lane == 64, squares, vel).reshape(own_z, 2, tok, 128)
        for i in range(own_z):
            pay[c, 0, i] = payload[i, 0]
            pay[c, 1, i] = payload[i, 1]
        y_copy(c).start()

    def share_out(c):
        y_copy(c).wait_recv()
        total = (pay[c, y] + y_recv[c]).reshape(own_z * tok, 128)
        summed = split_squares(total, sum_squares_lanes(total)).reshape(own_z, tok, 128)
        for i in range(own_z):
            z_send[c, i] = summed[i]

            @pl.when(c * own_z + i == z)
            def _():
                z_recv[z] = summed[i]

            @pl.when(c * own_z + i != z)
            def _():
                z_copy(c, i).start()

    @pl.loop(0, SKEW * (n_chunks - 1) + half + 3)
    def _(slot):
        @pl.loop(0, n_chunks)
        def _(c):
            step = slot - SKEW * c

            @pl.when(step == 0)
            def _():
                attend(c)
                ring_full(c, 1, 0).start()
                ring_full(c, 1, 1).start()
                acc[c] = jnp.dot(wbuf[z], att[z, c], preferred_element_type=F32)

            @pl.when(jnp.logical_and(step >= 1, step < half))
            def _():
                ring_full(c, step, 0).wait_recv()
                ring_full(c, step, 1).wait_recv()

                @pl.when(step < half - 1)
                def _():
                    ring_full(c, step + 1, 0).start()
                    ring_full(c, step + 1, 1).start()

                @pl.when(step == half - 1)
                def _():
                    ring_half(c, step + 1, 0).start()
                    ring_half(c, step + 1, 1).start()

                low = (z + n_z - step) % n_z
                high = (z + step) % n_z
                weights = jnp.concatenate([wbuf[low], wbuf[high]], axis=1)
                blocks = jnp.concatenate([att[low, c], att[high, c]], axis=0)
                acc[c] += jnp.dot(weights, blocks, preferred_element_type=F32)

            @pl.when(step == half)
            def _():
                ring_half(c, step, 0).wait_recv()
                ring_half(c, step, 1).wait_recv()
                far = (z + half) % n_z
                acc[c] += jnp.dot(wbuf[far], att[far, c], preferred_element_type=F32)
                rs_send[c] = acc[c, rows : 2 * rows].astype(BF16)
                rs_copy(c).start()

            @pl.when(step == half + 1)
            def _():
                finish_block(c)

            @pl.when(step == half + 2)
            def _():
                share_out(c)

    whole(z_recv.at[pl.ds(0, n_z - 1)], z_rsem).wait()
    total = z_recv[0].astype(F32)
    for i in range(1, n_z):
        total = total + z_recv[i].astype(F32)
    velocity = (total * lax.rsqrt(sum_squares_lanes(total) / d_out + 1e-06))[:, 0:64]
    vel_ref[...] = velocity
    level = jnp.full(velocity.shape, lev_ref[0].astype(F32), F32)
    delta = sigma_of(level + 1.0) - sigma_of(level)
    n_send[:, 0:64] = lat_ref[...] + delta * velocity
    n_send[:, 64:128] = jnp.zeros_like(velocity)
    onward = pltpu.make_async_remote_copy(
        src_ref=n_send, dst_ref=n_recv, send_sem=n_ssem, recv_sem=n_rsem, device_id=(after, me), device_id_type=MESH
    )
    onward.start()

    whole(qkv.at[pl.ds(1, 2), pl.ds(0, others)], kv_send).wait()
    whole(qkv.at[pl.ds(0, 1), pl.ds(0, others)], q_send).wait()
    whole(wbuf.at[:, pl.ds(rows, rows)], w_send).wait()

    @pl.loop(0, n_chunks)
    def _(c):
        @pl.loop(1, half)
        def _(step):
            ring_full(c, step, 0).wait_send()
            ring_full(c, step, 1).wait_send()

        ring_half(c, half, 0).wait_send()
        ring_half(c, half, 1).wait_send()
        rs_copy(c).wait_send()
        y_copy(c).wait_send()
        for i in range(own_z):

            @pl.when(c * own_z + i != z)
            def _():
                z_copy(c, i).wait_send()

    onward.wait()
    next_ref[...] = jnp.where(group == 0, fresh_ref[...], n_recv[:, 0:64])


def solution(mesh):
    n_queue, n_seq = mesh.shape["queue"], mesh.shape["seq"]
    n_z = n_seq // 2
    n_chunks = 4 if n_z >= 8 else 2

    def on_device(projected, out_weight, head_weight, hidden_in, latent, fresh_noise, levels):
        tok, width = projected.shape[1:]
        hd = width // n_seq
        rows, n_tok = hidden_in.shape
        chunk = n_tok // n_chunks
        own_z = n_z // n_chunks
        half = n_z // 2
        vmem = pl.BlockSpec(memory_space=pltpu.VMEM)
        hbm = pl.BlockSpec(memory_space=pl.ANY)
        dma = pltpu.SemaphoreType.DMA
        return pl.pallas_call(
            functools.partial(kernel, n_queue, n_z, n_chunks, rows * n_seq),
            out_shape=(
                jax.ShapeDtypeStruct((rows, n_tok), F32),
                jax.ShapeDtypeStruct((tok, 64), F32),
                jax.ShapeDtypeStruct((tok, 64), F32),
            ),
            in_specs=[hbm, hbm, vmem, vmem, vmem, vmem, pl.BlockSpec(memory_space=pltpu.SMEM)],
            out_specs=(vmem, vmem, vmem),
            scratch_shapes=[
                pltpu.VMEM((3, tok, width), BF16),
                pltpu.VMEM((3, n_tok, hd), BF16),
                pltpu.VMEM((hd, n_tok), BF16),
                pltpu.VMEM((n_tok, chunk), F32),
                pltpu.VMEM((n_z, n_chunks, hd, chunk), BF16),
                pltpu.VMEM((n_z, 2 * rows, hd), BF16),
                pltpu.VMEM((n_chunks, 2 * rows, chunk), F32),
                pltpu.VMEM((rows, 128), BF16),
                pltpu.VMEM((n_chunks, rows, chunk), BF16),
                pltpu.VMEM((n_chunks, rows, chunk), BF16),
                pltpu.VMEM((n_chunks, 2, own_z, tok, 128), F32),
                pltpu.VMEM((n_chunks, own_z, tok, 128), F32),
                pltpu.VMEM((n_chunks, own_z, tok, 128), BF16),
                pltpu.VMEM((n_z, tok, 128), BF16),
                pltpu.VMEM((tok, 128), F32),
                pltpu.VMEM((tok, 128), F32),
                dma, dma, dma, dma, dma, dma, dma, dma, dma,
                dma((2, n_chunks, half + 1)),
                dma((2, n_chunks, half + 1)),
                dma((n_chunks,)),
                dma((n_chunks,)),
                dma((n_chunks,)),
                dma((n_chunks,)),
                dma((n_chunks, own_z)),
                dma,
                dma,
                dma,
            ],
            compiler_params=pltpu.CompilerParams(
                collective_id=0, has_side_effects=True, vmem_limit_bytes=48 * 1024 * 1024
            ),
        )(projected, out_weight, head_weight, hidden_in, latent, fresh_noise, levels)

    return jax.shard_map(
        on_device,
        mesh=mesh,
        in_specs=(
            P(None, ("queue", "seq"), None),
            P("seq", None),
            P("seq", None),
            P("seq", "queue"),
            P(("queue", "seq"), None),
            P("seq", None),
            P("queue"),
        ),
        out_specs=(P("seq", "queue"), P(("queue", "seq"), None), P(("queue", "seq"), None)),
        check_vma=False,
    )
```

time: 683 us -> 183 us (0.27)
  waiting for transfers between devices: 504 us -> 0 us
  Pallas kernels: 0 us -> 173 us
  blocking collectives: 49.7 us -> 0 us
  starting transfers between devices: 46.3 us -> 0 us
  local copies, waits for them, and re-layouts: 46.6 us -> 8.12 us
  matrix products: 17.1 us -> 0 us
  between operations: 14.9 us -> 1.3 us
    all_gather x1 -> x0, waiting for transfers between devices: 304 us -> none  [on_device(): lax.all_gather(results, 'seq', axis=1, tiled=True)]
    pallas_call x0 -> x1, Pallas kernels: none -> 173 us  [on_device(): pl.pallas_call(functools.partial(kernel, n_queue, n_z, n_chunks, rows * n...]
    reduce_scatter x1 -> x0, waiting for transfers between devices: 140 us -> none  [on_device(): lax.psum_scatter(lax.dot_general(normed, head_weight, (((0,), (0,)), ((),...]
    all_to_all x1 -> x0, waiting for transfers between devices: 58.4 us -> none  [on_device(): lax.all_to_all(projected, 'seq', split_axis=2, concat_axis=1, tiled=True)]
    psum x1 -> x0, blocking collectives: 49.7 us -> none  [on_device(): squares = lax.psum(jnp.sum(block_out * block_out, axis=0), 'seq')]
    ppermute x1 -> x0, starting transfers between devices: 29.2 us -> none  [from_behind(): return lax.ppermute(block, axis, route)]
    slice x4 -> x0, local copies, waits for them, and re-layouts: 24.8 us -> none  [on_device(): results = attend(head_view[0, :, 0], head_view[1, :, 0], head_view[2, :, 0])]
    dot_general x8 -> x0, matrix products: 17.1 us -> none  [the longest x1 8.89 us: contract_last(): lax.dot_general(weight, rows, (((1,), (1,)), ((), ())), preferred_element...]
  transfers between devices with their start and end apart: 4 -> 0, of which waited for: 4 -> 0; matrix products, arithmetic and copies ran while one was open for 0% -> 0% of each run, Pallas kernels for 0% -> 0%
where the time goes in v1:
time: 183 us
  Pallas kernels  173 us (95%)
  local copies, waits for them, and re-layouts  8.12 us (4%)
    pallas_call x1, Pallas kernels, on_device(): pl.pallas_call(functools.partial(kernel, n_queue, n_z, n_chunks, rows * n...  173 us
    unnamed x14, local copies, waits for them, and re-layouts  8.12 us

profile of v1, /device:TPU:1, one launch (start us, length us, event | category | flops | bytes accessed | tf_op | source)
XLA Modules:
  0.0 182.7 jit_solution(12845474096809953978)
XLA Ops:
  1.3 0.9 copy.10.hw_ref
  2.1 0.0 copy-start
  2.2 1.3 copy-done
  3.5 0.0 copy-start.1
  3.5 1.3 copy-done.1
  4.7 0.0 copy-start.2
  4.7 1.0 copy-done.2
  5.8 0.0 copy-start.3
  5.8 0.7 copy-done.3
  6.5 0.0 copy-start.4
  6.5 0.7 copy-done.4
  7.2 173.3 %shard_map.94 = (f32[160,1536]{1,0:T(8,128)S(1)}, f32[48,64]{1,0:T(8,128)S(1)}, f32[48,64]{1,0:T(8,128)S(1)}) custom-call(bf16[3,48,4096]{2,1,0:T(8,128)(2,1)S(1)} %copy-done.1, bf16[160,4096]{1,0:T(8,128)(2,1)S(1)} %copy-done, bf16[160,64]{1,0:T(8,128)(2,1)S(1)} %copy.10.hw_ref, bf16[160,1536]{1,0:T(8,128)(2,1)S(1)} %copy-done.2, f32[48,64]{1,0:T(8,128)S(1)} %copy-done.3, ...), custom_call_target="tpu_custom_call" | custom-call | tf_op jit(solution)/shard_map/pallas_call | solution.py:353
  180.5 0.9 copy.15
  181.5 0.6 copy.16
  182.1 0.6 copy.17
Async XLA Ops:
  2.1 1.3 copy-start
  3.5 1.3 copy-start.1
  4.7 1.0 copy-start.2
  5.8 0.7 copy-start.3
  6.5 0.7 copy-start.4

commit v2 on v1

v2 whole, which is shorter than its diff:
```python
import functools
import math

import jax
import jax.numpy as jnp
from jax import lax
from jax.experimental import pallas as pl
from jax.experimental.pallas import tpu as pltpu
from jax.sharding import PartitionSpec as P

MESH = pl.DeviceIdType.MESH
F32 = jnp.float32
BF16 = jnp.bfloat16
STEPS = 50
SKEW = 1
LOG2E = 1.4426950408889634


def contract_last(a, b):
    return lax.dot_general(a, b, (((1,), (1,)), ((), ())), preferred_element_type=F32)


def sigma_of(level):
    frac = 1.0 - level / STEPS
    return 5.0 * frac / (1.0 + 4.0 * frac)


def kernel(
    n_queue, n_z, n_chunks, d_out,
    proj_hbm, w_hbm, hw_hbm, hid_hbm, lat_hbm, fresh_hbm, lev_ref,
    out_ref, vel_ref, next_ref,
    projv, qkv, vt, scores, att, wbuf, acc, hw_ref, hid_ref, lat_ref, fresh_ref, hwp, rs_send, rs_recv,
    sq_send, sq_recv, sq_column, pay, y_recv, z_send, z_recv, n_send, n_recv,
    proj_sem, small_sem, own_sem, kv_send, kv_recv, q_send, q_recv, w_own, w_send, w_recv, hw_send, hw_recv,
    ag_send, ag_recv, rs_ssem, rs_rsem, sq_ssem, sq_rsem, y_ssem, y_rsem, z_ssem, z_rsem, n_ssem, n_rsem,
):
    n_seq = 2 * n_z
    half = n_z // 2
    tok = projv.shape[1]
    hd = qkv.shape[2]
    n_tok = qkv.shape[1]
    chunk = n_tok // n_chunks
    lanes = math.gcd(chunk, 128)
    parts = chunk // lanes
    own_z = n_z // n_chunks
    rows = hid_ref.shape[0]
    group = lax.axis_index("queue")
    me = lax.axis_index("seq")
    z = me // 2
    y = me % 2
    partner = 2 * z + (1 - y)
    after = (group + 1) % n_queue
    before = (group + n_queue - 1) % n_queue

    barrier = pltpu.get_barrier_semaphore()
    load = pltpu.make_async_copy(proj_hbm, projv, proj_sem)
    load.start()

    @pl.loop(1, n_seq)
    def _(i):
        pl.semaphore_signal(barrier, inc=1, device_id=(group, (me + i) % n_seq), device_id_type=MESH)

    pl.semaphore_signal(barrier, inc=1, device_id=(after, me), device_id_type=MESH)
    pl.semaphore_signal(barrier, inc=1, device_id=(before, me), device_id_type=MESH)

    small = [
        pltpu.make_async_copy(src, dst, small_sem.at[i])
        for i, (src, dst) in enumerate(
            ((hw_hbm, hw_ref), (hid_hbm, hid_ref), (lat_hbm, lat_ref), (fresh_hbm, fresh_ref))
        )
    ]
    for copy in small:
        copy.start()

    @pl.loop(0, n_z)
    def _(i):
        pltpu.make_async_copy(
            w_hbm.at[:, pl.ds(pl.multiple_of((2 * i + y) * hd, hd), hd)], wbuf.at[i, pl.ds(0, rows)], w_own
        ).start()

    load.wait()
    small[0].wait()
    hwp[0:rows, 0:64] = hw_ref[...]
    hwp[0:rows, 64:128] = hw_ref[...]
    pl.semaphore_wait(barrier, n_seq + 1)

    def exchange(first, count, send_sem, recv_sem):
        def to(dest):
            pltpu.make_async_remote_copy(
                src_ref=projv.at[pl.ds(first, count), :, pl.ds(pl.multiple_of(dest * hd, hd), hd)],
                dst_ref=qkv.at[pl.ds(first, count), pl.ds(pl.multiple_of(me * tok, tok), tok), :],
                send_sem=send_sem,
                recv_sem=recv_sem,
                device_id=(group, dest),
                device_id_type=MESH,
            ).start()

        to(partner)

        @pl.loop(1, n_z)
        def _(i):
            far = n_z // 2 - i // 2
            shift = (1 - i % 2) * far + (i % 2) * (n_z - far)
            there = (z + shift) % n_z
            to(2 * there + y)
            to(2 * there + (1 - y))

    exchange(1, 2, kv_send, kv_recv)
    exchange(0, 1, q_send, q_recv)
    own = pltpu.make_async_copy(
        projv.at[:, :, pl.ds(pl.multiple_of(me * hd, hd), hd)],
        qkv.at[:, pl.ds(pl.multiple_of(me * tok, tok), tok), :],
        own_sem,
    )
    own.start()

    @pl.loop(0, n_z)
    def _(i):
        pltpu.make_async_remote_copy(
            src_ref=w_hbm.at[:, pl.ds(pl.multiple_of((2 * i + 1 - y) * hd, hd), hd)],
            dst_ref=wbuf.at[i, pl.ds(rows, rows)],
            send_sem=w_send,
            recv_sem=w_recv,
            device_id=(group, partner),
            device_id_type=MESH,
        ).start()

    hw_copy = pltpu.make_async_remote_copy(
        src_ref=hwp.at[pl.ds(0, rows)],
        dst_ref=hwp.at[pl.ds(rows, rows)],
        send_sem=hw_send,
        recv_sem=hw_recv,
        device_id=(group, partner),
        device_id_type=MESH,
    )
    hw_copy.start()

    def whole(ref, sem):
        return pltpu.make_async_copy(ref, ref, sem)

    others = (n_seq - 1) * tok
    for copy in small[1:]:
        copy.wait()
    own.wait()
    whole(qkv.at[pl.ds(1, 2), pl.ds(0, others)], kv_recv).wait()
    vt[...] = qkv[2].T
    whole(wbuf.at[:, pl.ds(0, rows)], w_own).wait()
    whole(wbuf.at[:, pl.ds(rows, rows)], w_recv).wait()
    hw_copy.wait_recv()
    whole(qkv.at[pl.ds(0, 1), pl.ds(0, others)], q_recv).wait()

    def ring(c, part, step, way):
        origin = (z + n_z - (step - 1)) % n_z if way == 0 else (z + step - 1) % n_z
        there = (z + 1) % n_z if way == 0 else (z + n_z - 1) % n_z

        def made(first, count):
            block = att.at[origin, c, pl.ds(first, count), pl.ds(part * lanes, lanes)]
            return pltpu.make_async_remote_copy(
                src_ref=block,
                dst_ref=block,
                send_sem=ag_send.at[way, c, part, step],
                recv_sem=ag_recv.at[way, c, part, step],
                device_id=(group, 2 * there + y),
                device_id_type=MESH,
            )

        return made

    def ring_full(c, part, step, way):
        return ring(c, part, step, way)(0, hd)

    def ring_half(c, part, step, way):
        return ring(c, part, step, way)(way * (hd // 2), hd // 2)

    key_block = math.gcd(256, n_tok)

    def attend(c):
        queries = qkv[0, pl.ds(pl.multiple_of(c * chunk, 16), chunk), :]
        peak = jnp.full((8, chunk), -jnp.inf, F32)
        for k in range(0, n_tok, key_block):
            part = contract_last(qkv[1, k : k + key_block, :], queries)
            scores[k : k + key_block, :] = part
            peak = jnp.maximum(peak, jnp.max(part.reshape(key_block // 8, 8, chunk), axis=0))
        peak = jnp.max(peak, axis=0, keepdims=True)
        total = jnp.zeros((8, chunk), F32)
        mixed = jnp.zeros((hd, chunk), F32)
        factor = LOG2E * hd ** (-0.5)
        for k in range(0, n_tok, key_block):
            raw = jnp.exp2((scores[k : k + key_block, :] - peak) * factor)
            total = total + jnp.sum(raw.reshape(key_block // 8, 8, chunk), axis=0)
            mixed = mixed + jnp.dot(vt[:, k : k + key_block], raw.astype(BF16), preferred_element_type=F32)
        total = jnp.sum(total, axis=0, keepdims=True)
        att[z, c] = (mixed / total).astype(BF16)

    def rs_copy(c, part):
        columns = pl.ds(part * lanes, lanes)
        return pltpu.make_async_remote_copy(
            src_ref=rs_send.at[c, :, columns],
            dst_ref=rs_recv.at[c, :, columns],
            send_sem=rs_ssem.at[c, part],
            recv_sem=rs_rsem.at[c, part],
            device_id=(group, partner),
            device_id_type=MESH,
        )

    def sq_copy(c, i):
        return pltpu.make_async_remote_copy(
            src_ref=sq_send.at[c],
            dst_ref=sq_recv.at[me],
            send_sem=sq_ssem.at[c, i],
            recv_sem=sq_rsem,
            device_id=(group, c * (2 * own_z) + i),
            device_id_type=MESH,
        )

    def y_copy(c):
        return pltpu.make_async_remote_copy(
            src_ref=pay.at[c, 1 - y],
            dst_ref=y_recv.at[c],
            send_sem=y_ssem.at[c],
            recv_sem=y_rsem.at[c],
            device_id=(group, partner),
            device_id_type=MESH,
        )

    def z_copy(c, i):
        return pltpu.make_async_remote_copy(
            src_ref=z_send.at[c, i],
            dst_ref=z_recv.at[z],
            send_sem=z_ssem.at[c, i],
            recv_sem=z_rsem,
            device_id=(group, 2 * (c * own_z + i) + y),
            device_id_type=MESH,
        )

    def part_velocity(c):
        turned = acc[c].T
        upper = turned.astype(BF16)
        lower = (turned - upper.astype(F32)).astype(BF16)
        vel = jnp.dot(upper, hwp[...], preferred_element_type=F32) + jnp.dot(lower, hwp[...], preferred_element_type=F32)
        vel = vel.reshape(own_z, 2, 2, tok // 2, 128)
        lane = lax.broadcasted_iota(jnp.int32, (tok // 2, 128), 1)
        for i in range(own_z):
            for k in range(2):
                pay[c, k, i] = jnp.where(lane < 64, vel[i, k, 0], vel[i, k, 1])
        y_copy(c).start()

    def finish_block(c):
        for part in range(parts):
            rs_copy(c, part).wait_recv()
            here = slice(part * lanes, (part + 1) * lanes)
            x = acc[c, 0:rows, here] + rs_recv[c, :, here].astype(F32)
            out_ref[:, pl.ds(pl.multiple_of(c * chunk + part * lanes, lanes), lanes)] = x
            sq_send[c, :, here] = jnp.sum(x * x, axis=0, keepdims=True)

        for i in range(2 * own_z):

            @pl.when(c * (2 * own_z) + i == me)
            def _():
                sq_recv[me] = sq_send[c]

            @pl.when(c * (2 * own_z) + i != me)
            def _():
                sq_copy(c, i).start()

    def share_out(c):
        y_copy(c).wait_recv()
        for i in range(own_z):
            total = pay[c, y, i] + y_recv[c, i]
            z_send[c, i] = total

            @pl.when(c * own_z + i == z)
            def _():
                z_recv[z] = total

            @pl.when(c * own_z + i != z)
            def _():
                z_copy(c, i).start()

    @pl.loop(0, SKEW * (n_chunks - 1) + half + 3)
    def _(slot):
        @pl.loop(0, n_chunks)
        def _(c):
            step = slot - SKEW * c

            @pl.when(step == 0)
            def _():
                attend(c)
                for part in range(parts):
                    ring_full(c, part, 1, 0).start()
                    ring_full(c, part, 1, 1).start()
                first = jnp.dot(wbuf[z], att[z, c], preferred_element_type=F32)
                columns = pl.ds(pl.multiple_of(c * chunk, chunk), chunk)
                acc[c, 0:rows] = first[0:rows] + hid_ref[:, columns].astype(F32)
                acc[c, rows : 2 * rows] = first[rows : 2 * rows]

            @pl.when(jnp.logical_and(step >= 1, step < half))
            def _():
                for part in range(parts):
                    for way in range(2):
                        ring_full(c, part, step, way).wait_recv()

                        @pl.when(step < half - 1)
                        def _():
                            ring_full(c, part, step + 1, way).start()

                        @pl.when(step == half - 1)
                        def _():
                            ring_half(c, part, step + 1, way).start()

                low = (z + n_z - step) % n_z
                high = (z + step) % n_z
                weights = jnp.concatenate([wbuf[low], wbuf[high]], axis=1)
                blocks = jnp.concatenate([att[low, c], att[high, c]], axis=0)
                acc[c] += jnp.dot(weights, blocks, preferred_element_type=F32)

            @pl.when(step == half)
            def _():
                far = (z + half) % n_z
                for part in range(parts):
                    ring_half(c, part, step, 0).wait_recv()
                    ring_half(c, part, step, 1).wait_recv()
                    here = slice(part * lanes, (part + 1) * lanes)
                    last = acc[c, :, here] + jnp.dot(wbuf[far], att[far, c, :, here], preferred_element_type=F32)
                    acc[c, :, here] = last
                    rs_send[c, :, here] = last[rows : 2 * rows].astype(BF16)
                    rs_copy(c, part).start()
                part_velocity(c)

            @pl.when(step == half + 1)
            def _():
                finish_block(c)

            @pl.when(step == half + 2)
            def _():
                share_out(c)

    whole(z_recv.at[pl.ds(0, n_z - 1)], z_rsem).wait()
    total = z_recv[0]
    for i in range(1, n_z):
        total = total + z_recv[i]
    whole(sq_recv.at[pl.ds(0, n_seq - 1)], sq_rsem).wait()
    squares = jnp.sum(sq_recv[...], axis=0)
    sq_column[...] = jnp.broadcast_to(lax.rsqrt(squares / d_out + 1e-06), (128, chunk)).T
    scale = sq_column[pl.ds(pl.multiple_of(me % (2 * own_z) * tok, 8), tok), 0:64]
    velocity = jnp.concatenate([total[:, 0:64], total[:, 64:128]], axis=0) * scale
    vel_ref[...] = velocity
    level = jnp.full(velocity.shape, lev_ref[0].astype(F32), F32)
    delta = sigma_of(level + 1.0) - sigma_of(level)
    n_send[:, 0:64] = lat_ref[...] + delta * velocity
    n_send[:, 64:128] = jnp.zeros_like(velocity)
    onward = pltpu.make_async_remote_copy(
        src_ref=n_send, dst_ref=n_recv, send_sem=n_ssem, recv_sem=n_rsem, device_id=(after, me), device_id_type=MESH
    )
    onward.start()

    whole(qkv.at[pl.ds(1, 2), pl.ds(0, others)], kv_send).wait()
    whole(qkv.at[pl.ds(0, 1), pl.ds(0, others)], q_send).wait()
    whole(wbuf.at[:, pl.ds(rows, rows)], w_send).wait()
    hw_copy.wait_send()

    @pl.loop(0, n_chunks)
    def _(c):
        for part in range(parts):

            @pl.loop(1, half)
            def _(step):
                ring_full(c, part, step, 0).wait_send()
                ring_full(c, part, step, 1).wait_send()

            ring_half(c, part, half, 0).wait_send()
            ring_half(c, part, half, 1).wait_send()
            rs_copy(c, part).wait_send()
        y_copy(c).wait_send()
        for i in range(own_z):

            @pl.when(c * own_z + i != z)
            def _():
                z_copy(c, i).wait_send()

        for i in range(2 * own_z):

            @pl.when(c * (2 * own_z) + i != me)
            def _():
                sq_copy(c, i).wait_send()

    onward.wait()
    next_ref[...] = jnp.where(group == 0, fresh_ref[...], n_recv[:, 0:64])


def solution(mesh):
    n_queue, n_seq = mesh.shape["queue"], mesh.shape["seq"]
    n_z = n_seq // 2
    n_chunks = 4 if n_z >= 8 else 2

    def on_device(projected, out_weight, head_weight, hidden_in, latent, fresh_noise, levels):
        tok, width = projected.shape[1:]
        hd = width // n_seq
        rows, n_tok = hidden_in.shape
        chunk = n_tok // n_chunks
        own_z = n_z // n_chunks
        half = n_z // 2
        parts = chunk // math.gcd(chunk, 128)
        vmem = pl.BlockSpec(memory_space=pltpu.VMEM)
        hbm = pl.BlockSpec(memory_space=pltpu.HBM)
        dma = pltpu.SemaphoreType.DMA
        return pl.pallas_call(
            functools.partial(kernel, n_queue, n_z, n_chunks, rows * n_seq),
            out_shape=(
                jax.ShapeDtypeStruct((rows, n_tok), F32),
                jax.ShapeDtypeStruct((tok, 64), F32),
                jax.ShapeDtypeStruct((tok, 64), F32),
            ),
            in_specs=[hbm, hbm, hbm, hbm, hbm, hbm, pl.BlockSpec(memory_space=pltpu.SMEM)],
            out_specs=(vmem, vmem, vmem),
            scratch_shapes=[
                pltpu.VMEM((3, tok, width), BF16),
                pltpu.VMEM((3, n_tok, hd), BF16),
                pltpu.VMEM((hd, n_tok), BF16),
                pltpu.VMEM((n_tok, chunk), F32),
                pltpu.VMEM((n_z, n_chunks, hd, chunk), BF16),
                pltpu.VMEM((n_z, 2 * rows, hd), BF16),
                pltpu.VMEM((n_chunks, 2 * rows, chunk), F32),
                pltpu.VMEM((rows, 64), BF16),
                pltpu.VMEM((rows, n_tok), BF16),
                pltpu.VMEM((tok, 64), F32),
                pltpu.VMEM((tok, 64), F32),
                pltpu.VMEM((2 * rows, 128), BF16),
                pltpu.VMEM((n_chunks, rows, chunk), BF16),
                pltpu.VMEM((n_chunks, rows, chunk), BF16),
                pltpu.VMEM((n_chunks, 1, chunk), F32),
                pltpu.VMEM((n_seq, 1, chunk), F32),
                pltpu.VMEM((chunk, 128), F32),
                pltpu.VMEM((n_chunks, 2, own_z, tok // 2, 128), F32),
                pltpu.VMEM((n_chunks, own_z, tok // 2, 128), F32),
                pltpu.VMEM((n_chunks, own_z, tok // 2, 128), F32),
                pltpu.VMEM((n_z, tok // 2, 128), F32),
                pltpu.VMEM((tok, 128), F32),
                pltpu.VMEM((tok, 128), F32),
                dma, dma((4,)), dma, dma, dma, dma, dma, dma, dma, dma, dma, dma,
                dma((2, n_chunks, parts, half + 1)),
                dma((2, n_chunks, parts, half + 1)),
                dma((n_chunks, parts)),
                dma((n_chunks, parts)),
                dma((n_chunks, 2 * own_z)),
                dma,
                dma((n_chunks,)),
                dma((n_chunks,)),
                dma((n_chunks, own_z)),
                dma,
                dma,
                dma,
            ],
            compiler_params=pltpu.CompilerParams(
                collective_id=0, has_side_effects=True, vmem_limit_bytes=48 * 1024 * 1024
            ),
        )(projected, out_weight, head_weight, hidden_in, latent, fresh_noise, levels)

    return jax.shard_map(
        on_device,
        mesh=mesh,
        in_specs=(
            P(None, ("queue", "seq"), None),
            P("seq", None),
            P("seq", None),
            P("seq", "queue"),
            P(("queue", "seq"), None),
            P("seq", None),
            P("queue"),
        ),
        out_specs=(P("seq", "queue"), P(("queue", "seq"), None), P(("queue", "seq"), None)),
        check_vma=False,
    )
```

time: 183 us -> 168 us (0.918)
  Pallas kernels: 173 us -> 158 us
    pallas_call x1, Pallas kernels: 173 us -> 158 us  [on_device(): pl.pallas_call(functools.partial(kernel, n_queue, n_z, n_chunks, rows * n...]
where the time goes in v2:
time: 168 us; the launch traced here: 167 us
  Pallas kernels  158 us (94%)
  local copies, waits for them, and re-layouts  8.12 us (5%)
    pallas_call x1, Pallas kernels, on_device(): pl.pallas_call(functools.partial(kernel, n_queue, n_z, n_chunks, rows * n...  158 us
    unnamed x14, local copies, waits for them, and re-layouts  8.12 us

profile of v2, /device:TPU:1, one launch (start us, length us, event | category | flops | bytes accessed | tf_op | source)
XLA Modules:
  0.0 167.3 jit_solution(6417596872946869094)
XLA Ops:
  1.3 0.9 copy.10.hw_hbm
  2.1 0.0 copy-start
  2.2 1.3 copy-done
  3.5 0.0 copy-start.1
  3.5 1.3 copy-done.1
  4.7 0.0 copy-start.2
  4.7 1.0 copy-done.2
  5.8 0.0 copy-start.3
  5.8 0.7 copy-done.3
  6.5 0.0 copy-start.4
  6.5 0.7 copy-done.4
  7.2 157.9 %shard_map.94 = (f32[160,1536]{1,0:T(8,128)S(1)}, f32[48,64]{1,0:T(8,128)S(1)}, f32[48,64]{1,0:T(8,128)S(1)}) custom-call(bf16[3,48,4096]{2,1,0:T(8,128)(2,1)S(1)} %copy-done.1, bf16[160,4096]{1,0:T(8,128)(2,1)S(1)} %copy-done, bf16[160,64]{1,0:T(8,128)(2,1)S(1)} %copy.10.hw_hbm, bf16[160,1536]{1,0:T(8,128)(2,1)S(1)} %copy-done.2, f32[48,64]{1,0:T(8,128)S(1)} %copy-done.3, ...), custom_call_target="tpu_custom_call" | custom-call | tf_op jit(solution)/shard_map/pallas_call | solution.py:407
  165.2 0.9 copy.15
  166.1 0.6 copy.16
  166.7 0.6 copy.17
Async XLA Ops:
  2.1 1.3 copy-start
  3.5 1.3 copy-start.1
  4.7 1.0 copy-start.2
  5.8 0.7 copy-start.3
  6.5 0.7 copy-start.4

commit v3 on v2

--- a/solution.py
+++ b/solution.py
@@ -12,7 +12,7 @@
 F32 = jnp.float32
 BF16 = jnp.bfloat16
 STEPS = 50
-SKEW = 1
+PAIR = 2
 LOG2E = 1.4426950408889634
 
 
@@ -80,8 +80,9 @@
 
     load.wait()
     small[0].wait()
-    hwp[0:rows, 0:64] = hw_ref[...]
-    hwp[0:rows, 64:128] = hw_ref[...]
+    heads = hw_ref[...].astype(F32).T.astype(BF16)
+    hwp[0:rows, 0:64] = heads
+    hwp[0:rows, 64:128] = heads
     pl.semaphore_wait(barrier, n_seq + 1)
 
     def exchange(first, count, send_sem, recv_sem):
@@ -158,8 +159,8 @@
             return pltpu.make_async_remote_copy(
                 src_ref=block,
                 dst_ref=block,
-                send_sem=ag_send.at[way, c, part, step],
-                recv_sem=ag_recv.at[way, c, part, step],
+                send_sem=ag_send.at[way],
+                recv_sem=ag_recv.at[way, c, part, step % 3],
                 device_id=(group, 2 * there + y),
                 device_id_type=MESH,
             )
@@ -197,7 +198,7 @@
         return pltpu.make_async_remote_copy(
             src_ref=rs_send.at[c, :, columns],
             dst_ref=rs_recv.at[c, :, columns],
-            send_sem=rs_ssem.at[c, part],
+            send_sem=rs_ssem,
             recv_sem=rs_rsem.at[c, part],
             device_id=(group, partner),
             device_id_type=MESH,
@@ -207,7 +208,7 @@
         return pltpu.make_async_remote_copy(
             src_ref=sq_send.at[c],
             dst_ref=sq_recv.at[me],
-            send_sem=sq_ssem.at[c, i],
+            send_sem=sq_ssem,
             recv_sem=sq_rsem,
             device_id=(group, c * (2 * own_z) + i),
             device_id_type=MESH,
@@ -217,7 +218,7 @@
         return pltpu.make_async_remote_copy(
             src_ref=pay.at[c, 1 - y],
             dst_ref=y_recv.at[c],
-            send_sem=y_ssem.at[c],
+            send_sem=y_ssem,
             recv_sem=y_rsem.at[c],
             device_id=(group, partner),
             device_id_type=MESH,
@@ -227,7 +228,7 @@
         return pltpu.make_async_remote_copy(
             src_ref=z_send.at[c, i],
             dst_ref=z_recv.at[z],
-            send_sem=z_ssem.at[c, i],
+            send_sem=z_ssem,
             recv_sem=z_rsem,
             device_id=(group, 2 * (c * own_z + i) + y),
             device_id_type=MESH,
@@ -267,21 +268,22 @@
         y_copy(c).wait_recv()
         for i in range(own_z):
             total = pay[c, y, i] + y_recv[c, i]
-            z_send[c, i] = total
+            padded = jnp.concatenate([total, jnp.zeros((8, 128), F32)], axis=0).astype(BF16)
+            z_send[c, i] = padded
 
             @pl.when(c * own_z + i == z)
             def _():
-                z_recv[z] = total
+                z_recv[z] = padded
 
             @pl.when(c * own_z + i != z)
             def _():
                 z_copy(c, i).start()
 
-    @pl.loop(0, SKEW * (n_chunks - 1) + half + 3)
+    @pl.loop(0, (n_chunks - 1) // PAIR + half + 3)
     def _(slot):
         @pl.loop(0, n_chunks)
         def _(c):
-            step = slot - SKEW * c
+            step = slot - c // PAIR
 
             @pl.when(step == 0)
             def _():
@@ -336,9 +338,10 @@
                 share_out(c)
 
     whole(z_recv.at[pl.ds(0, n_z - 1)], z_rsem).wait()
-    total = z_recv[0]
+    total = z_recv[0].astype(F32)
     for i in range(1, n_z):
-        total = total + z_recv[i]
+        total = total + z_recv[i].astype(F32)
+    total = total[0 : tok // 2]
     whole(sq_recv.at[pl.ds(0, n_seq - 1)], sq_rsem).wait()
     squares = jnp.sum(sq_recv[...], axis=0)
     sq_column[...] = jnp.broadcast_to(lax.rsqrt(squares / d_out + 1e-06), (128, chunk)).T
@@ -359,33 +362,25 @@
     whole(wbuf.at[:, pl.ds(rows, rows)], w_send).wait()
     hw_copy.wait_send()
 
-    @pl.loop(0, n_chunks)
-    def _(c):
-        for part in range(parts):
-
-            @pl.loop(1, half)
-            def _(step):
-                ring_full(c, part, step, 0).wait_send()
-                ring_full(c, part, step, 1).wait_send()
-
-            ring_half(c, part, half, 0).wait_send()
-            ring_half(c, part, half, 1).wait_send()
-            rs_copy(c, part).wait_send()
-        y_copy(c).wait_send()
-        for i in range(own_z):
-
-            @pl.when(c * own_z + i != z)
-            def _():
-                z_copy(c, i).wait_send()
-
-        for i in range(2 * own_z):
-
-            @pl.when(c * (2 * own_z) + i != me)
-            def _():
-                sq_copy(c, i).wait_send()
+    for way in range(2):
+        whole(att.at[pl.ds(0, half - 1)], ag_send.at[way]).wait()
+        whole(att.at[0, :, pl.ds(0, hd // 2)], ag_send.at[way]).wait()
+    whole(rs_recv, rs_ssem).wait()
+    whole(y_recv, y_ssem).wait()
+    whole(z_recv.at[pl.ds(0, n_z - 1)], z_ssem).wait()
+    whole(sq_recv.at[pl.ds(0, n_seq - 1)], sq_ssem).wait()
 
     onward.wait()
     next_ref[...] = jnp.where(group == 0, fresh_ref[...], n_recv[:, 0:64])
+
+
+def write_out(*refs):
+    sems = refs[6]
+    copies = [pltpu.make_async_copy(refs[i], refs[3 + i], sems.at[i]) for i in range(3)]
+    for copy in copies:
+        copy.start()
+    for copy in copies:
+        copy.wait()
 
 
 def solution(mesh):
@@ -404,12 +399,12 @@
         vmem = pl.BlockSpec(memory_space=pltpu.VMEM)
         hbm = pl.BlockSpec(memory_space=pltpu.HBM)
         dma = pltpu.SemaphoreType.DMA
-        return pl.pallas_call(
+        results = pl.pallas_call(
             functools.partial(kernel, n_queue, n_z, n_chunks, rows * n_seq),
             out_shape=(
-                jax.ShapeDtypeStruct((rows, n_tok), F32),
-                jax.ShapeDtypeStruct((tok, 64), F32),
-                jax.ShapeDtypeStruct((tok, 64), F32),
+                pltpu.VMEM((rows, n_tok), F32),
+                pltpu.VMEM((tok, 64), F32),
+                pltpu.VMEM((tok, 64), F32),
             ),
             in_specs=[hbm, hbm, hbm, hbm, hbm, hbm, pl.BlockSpec(memory_space=pltpu.SMEM)],
             out_specs=(vmem, vmem, vmem),
@@ -421,7 +416,7 @@
                 pltpu.VMEM((n_z, n_chunks, hd, chunk), BF16),
                 pltpu.VMEM((n_z, 2 * rows, hd), BF16),
                 pltpu.VMEM((n_chunks, 2 * rows, chunk), F32),
-                pltpu.VMEM((rows, 64), BF16),
+                pltpu.VMEM((64, rows), BF16),
                 pltpu.VMEM((rows, n_tok), BF16),
                 pltpu.VMEM((tok, 64), F32),
                 pltpu.VMEM((tok, 64), F32),
@@ -433,28 +428,35 @@
                 pltpu.VMEM((chunk, 128), F32),
                 pltpu.VMEM((n_chunks, 2, own_z, tok // 2, 128), F32),
                 pltpu.VMEM((n_chunks, own_z, tok // 2, 128), F32),
-                pltpu.VMEM((n_chunks, own_z, tok // 2, 128), F32),
-                pltpu.VMEM((n_z, tok // 2, 128), F32),
+                pltpu.VMEM((n_chunks, own_z, tok // 2 + 8, 128), BF16),
+                pltpu.VMEM((n_z, tok // 2 + 8, 128), BF16),
                 pltpu.VMEM((tok, 128), F32),
                 pltpu.VMEM((tok, 128), F32),
                 dma, dma((4,)), dma, dma, dma, dma, dma, dma, dma, dma, dma, dma,
-                dma((2, n_chunks, parts, half + 1)),
-                dma((2, n_chunks, parts, half + 1)),
+                dma((2,)),
+                dma((2, n_chunks, parts, 3)),
+                dma,
                 dma((n_chunks, parts)),
-                dma((n_chunks, parts)),
-                dma((n_chunks, 2 * own_z)),
+                dma,
+                dma,
                 dma,
                 dma((n_chunks,)),
-                dma((n_chunks,)),
-                dma((n_chunks, own_z)),
+                dma,
                 dma,
                 dma,
                 dma,
             ],
             compiler_params=pltpu.CompilerParams(
-                collective_id=0, has_side_effects=True, vmem_limit_bytes=48 * 1024 * 1024
+                collective_id=0, has_side_effects=True, vmem_limit_bytes=62 * 1024 * 1024
             ),
-        )(projected, out_weight, head_weight, hidden_in, latent, fresh_noise, levels)
+        )(projected, out_weight, head_weight.T, hidden_in, latent, fresh_noise, levels)
+        return pl.pallas_call(
+            write_out,
+            out_shape=tuple(jax.ShapeDtypeStruct(r.shape, r.dtype) for r in results),
+            in_specs=[vmem] * 3,
+            out_specs=(hbm, hbm, hbm),
+            scratch_shapes=[dma((3,))],
+        )(*results)
 
     return jax.shard_map(
         on_device,

time: 168 us -> 154 us (0.917)
  Pallas kernels: 158 us -> 150 us
  local copies, waits for them, and re-layouts: 8.12 us -> 2.16 us
    pallas_call x1, Pallas kernels: 158 us -> 148 us  [on_device(): pl.pallas_call(functools.partial(kernel, n_queue, n_z, n_chunks, rows * n...]
    unnamed x14 -> x6, local copies, waits for them, and re-layouts: 8.12 us -> 2.16 us
    pallas_call x0 -> x1, Pallas kernels: none -> 2.19 us  [on_device(): pl.pallas_call(write_out, out_shape=tuple((jax.ShapeDtypeStruct(r.shape,...]
where the time goes in v3:
time: 154 us
  Pallas kernels  150 us (97%)
  local copies, waits for them, and re-layouts  2.16 us (1%)
    pallas_call x1, Pallas kernels, on_device(): pl.pallas_call(functools.partial(kernel, n_queue, n_z, n_chunks, rows * n...  148 us

profile of v3, /device:TPU:1, one launch (start us, length us, event | category | flops | bytes accessed | tf_op | source)
XLA Modules:
  0.0 153.7 jit_solution(2559163051717180738)
XLA Ops:
  1.3 148.1 %shard_map.94 = (f32[160,1536]{1,0:T(8,128)S(1)}, f32[48,64]{1,0:T(8,128)S(1)}, f32[48,64]{1,0:T(8,128)S(1)}) custom-call(bf16[3,48,4096]{2,1,0:T(8,128)(2,1)} %proj_hbm.1, bf16[160,4096]{1,0:T(8,128)(2,1)} %w_hbm.1, bf16[64,160]{1,0:T(8,128)(2,1)} %bitcast.1, bf16[160,1536]{1,0:T(8,128)(2,1)} %hid_hbm.1, f32[48,64]{1,0:T(8,128)} %lat_hbm.1, ...), custom_call_target="tpu_custom_call" | custom-call | tf_op jit(solution)/shard_map/pallas_call | solution.py:402
  149.3 0.0 copy-start
  149.4 1.0 copy-done
  150.3 0.0 copy-start.1
  150.3 0.6 copy-done.1
  150.9 0.0 copy-start.2
  150.9 0.6 copy-done.2
  151.5 2.2 %shard_map.95 = (f32[160,1536]{1,0:T(8,128)}, f32[48,64]{1,0:T(8,128)}, f32[48,64]{1,0:T(8,128)}) custom-call(f32[160,1536]{1,0:T(8,128)} %copy-done, f32[48,64]{1,0:T(8,128)} %copy-done.1, f32[48,64]{1,0:T(8,128)} %copy-done.2), custom_call_target="tpu_custom_call" | custom-call | tf_op jit(solution)/shard_map/pallas_call | solution.py:453
Async XLA Ops:
  149.3 1.0 copy-start
  150.3 0.6 copy-start.1
  150.9 0.6 copy-start.2

commit v4 on v3

--- a/solution.py
+++ b/solution.py
@@ -204,10 +204,14 @@
             device_id_type=MESH,
         )
 
+    def lanes_of(i):
+        first = i * tok // lanes * lanes
+        return pl.ds(first, -(-(i + 1) * tok // lanes) * lanes - first)
+
     def sq_copy(c, i):
         return pltpu.make_async_remote_copy(
-            src_ref=sq_send.at[c],
-            dst_ref=sq_recv.at[me],
+            src_ref=sq_send.at[c, :, lanes_of(i)],
+            dst_ref=sq_recv.at[me, :, lanes_of(i)],
             send_sem=sq_ssem,
             recv_sem=sq_rsem,
             device_id=(group, c * (2 * own_z) + i),
@@ -342,7 +346,12 @@
     for i in range(1, n_z):
         total = total + z_recv[i].astype(F32)
     total = total[0 : tok // 2]
-    whole(sq_recv.at[pl.ds(0, n_seq - 1)], sq_rsem).wait()
+    for i in range(2 * own_z):
+
+        @pl.when(me % (2 * own_z) == i)
+        def _():
+            whole(sq_recv.at[pl.ds(0, n_seq - 1), :, lanes_of(i)], sq_rsem).wait()
+
     squares = jnp.sum(sq_recv[...], axis=0)
     sq_column[...] = jnp.broadcast_to(lax.rsqrt(squares / d_out + 1e-06), (128, chunk)).T
     scale = sq_column[pl.ds(pl.multiple_of(me % (2 * own_z) * tok, 8), tok), 0:64]
@@ -368,7 +377,16 @@
     whole(rs_recv, rs_ssem).wait()
     whole(y_recv, y_ssem).wait()
     whole(z_recv.at[pl.ds(0, n_z - 1)], z_ssem).wait()
-    whole(sq_recv.at[pl.ds(0, n_seq - 1)], sq_ssem).wait()
+    for i in range(2 * own_z):
+
+        @pl.when(me % (2 * own_z) != i)
+        def _():
+            whole(sq_recv.at[pl.ds(0, n_chunks), :, lanes_of(i)], sq_ssem).wait()
+
+        @pl.when(me % (2 * own_z) == i)
+        def _():
+            whole(sq_recv.at[pl.ds(0, n_chunks - 1), :, lanes_of(i)], sq_ssem).wait()
+
 
     onward.wait()
     next_ref[...] = jnp.where(group == 0, fresh_ref[...], n_recv[:, 0:64])
@@ -456,6 +474,7 @@
             in_specs=[vmem] * 3,
             out_specs=(hbm, hbm, hbm),
             scratch_shapes=[dma((3,))],
+            compiler_params=pltpu.CompilerParams(vmem_limit_bytes=4 * 1024 * 1024),
         )(*results)
 
     return jax.shard_map(

time: 154 us -> 150 us (0.974)
  local copies, waits for them, and re-layouts: 2.16 us -> 0 us
  Pallas kernels: 150 us -> 148 us
    unnamed x6 -> x0, local copies, waits for them, and re-layouts: 2.16 us -> none
where the time goes in v4:
time: 150 us
  Pallas kernels  148 us (99%)
    pallas_call x1, Pallas kernels, on_device(): pl.pallas_call(functools.partial(kernel, n_queue, n_z, n_chunks, rows * n...  147 us

profile of v4, /device:TPU:1, one launch (start us, length us, event | category | flops | bytes accessed | tf_op | source)
XLA Modules:
  0.0 149.7 jit_solution(17999156027115029013)
XLA Ops:
  1.3 147.4 %shard_map.94 = (f32[160,1536]{1,0:T(8,128)S(1)}, f32[48,64]{1,0:T(8,128)S(1)}, f32[48,64]{1,0:T(8,128)S(1)}) custom-call(bf16[3,48,4096]{2,1,0:T(8,128)(2,1)} %proj_hbm.1, bf16[160,4096]{1,0:T(8,128)(2,1)} %w_hbm.1, bf16[64,160]{1,0:T(8,128)(2,1)} %bitcast.1, bf16[160,1536]{1,0:T(8,128)(2,1)} %hid_hbm.1, f32[48,64]{1,0:T(8,128)} %lat_hbm.1, ...), custom_call_target="tpu_custom_call" | custom-call | tf_op jit(solution)/shard_map/pallas_call | solution.py:420
  148.7 1.0 shard_map.95

commit v5 on v4

--- a/solution.py
+++ b/solution.py
@@ -175,23 +175,23 @@
 
     key_block = math.gcd(256, n_tok)
 
-    def attend(c):
-        queries = qkv[0, pl.ds(pl.multiple_of(c * chunk, 16), chunk), :]
-        peak = jnp.full((8, chunk), -jnp.inf, F32)
+    def attend(c, part):
+        queries = qkv[0, pl.ds(pl.multiple_of(c * chunk + part * lanes, 16), lanes), :]
+        peak = jnp.full((8, lanes), -jnp.inf, F32)
         for k in range(0, n_tok, key_block):
-            part = contract_last(qkv[1, k : k + key_block, :], queries)
-            scores[k : k + key_block, :] = part
-            peak = jnp.maximum(peak, jnp.max(part.reshape(key_block // 8, 8, chunk), axis=0))
+            some = contract_last(qkv[1, k : k + key_block, :], queries)
+            scores[k : k + key_block, :] = some
+            peak = jnp.maximum(peak, jnp.max(some.reshape(key_block // 8, 8, lanes), axis=0))
         peak = jnp.max(peak, axis=0, keepdims=True)
-        total = jnp.zeros((8, chunk), F32)
-        mixed = jnp.zeros((hd, chunk), F32)
+        total = jnp.zeros((8, lanes), F32)
+        mixed = jnp.zeros((hd, lanes), F32)
         factor = LOG2E * hd ** (-0.5)
         for k in range(0, n_tok, key_block):
             raw = jnp.exp2((scores[k : k + key_block, :] - peak) * factor)
-            total = total + jnp.sum(raw.reshape(key_block // 8, 8, chunk), axis=0)
+            total = total + jnp.sum(raw.reshape(key_block // 8, 8, lanes), axis=0)
             mixed = mixed + jnp.dot(vt[:, k : k + key_block], raw.astype(BF16), preferred_element_type=F32)
         total = jnp.sum(total, axis=0, keepdims=True)
-        att[z, c] = (mixed / total).astype(BF16)
+        att[z, c, :, part * lanes : (part + 1) * lanes] = (mixed / total).astype(BF16)
 
     def rs_copy(c, part):
         columns = pl.ds(part * lanes, lanes)
@@ -291,8 +291,8 @@
 
             @pl.when(step == 0)
             def _():
-                attend(c)
                 for part in range(parts):
+                    attend(c, part)
                     ring_full(c, part, 1, 0).start()
                     ring_full(c, part, 1, 1).start()
                 first = jnp.dot(wbuf[z], att[z, c], preferred_element_type=F32)
@@ -430,7 +430,7 @@
                 pltpu.VMEM((3, tok, width), BF16),
                 pltpu.VMEM((3, n_tok, hd), BF16),
                 pltpu.VMEM((hd, n_tok), BF16),
-                pltpu.VMEM((n_tok, chunk), F32),
+                pltpu.VMEM((n_tok, math.gcd(chunk, 128)), F32),
                 pltpu.VMEM((n_z, n_chunks, hd, chunk), BF16),
                 pltpu.VMEM((n_z, 2 * rows, hd), BF16),
                 pltpu.VMEM((n_chunks, 2 * rows, chunk), F32),

time: 150 us -> 151 us (level); the launches traced: 150 us -> 149 us
  no operation moved by 1% of the time
where the time goes in v5:
time: 151 us; the launch traced here: 149 us
  Pallas kernels  148 us (98%)
    pallas_call x1, Pallas kernels, on_device(): pl.pallas_call(functools.partial(kernel, n_queue, n_z, n_chunks, rows * n...  147 us

profile of v5, /device:TPU:1, one launch (start us, length us, event | category | flops | bytes accessed | tf_op | source)
XLA Modules:
  0.0 149.1 jit_solution(16173795418698821392)
XLA Ops:
  1.3 146.8 %shard_map.94 = (f32[160,1536]{1,0:T(8,128)S(1)}, f32[48,64]{1,0:T(8,128)S(1)}, f32[48,64]{1,0:T(8,128)S(1)}) custom-call(bf16[3,48,4096]{2,1,0:T(8,128)(2,1)} %proj_hbm.1, bf16[160,4096]{1,0:T(8,128)(2,1)} %w_hbm.1, bf16[64,160]{1,0:T(8,128)(2,1)} %bitcast.1, bf16[160,1536]{1,0:T(8,128)(2,1)} %hid_hbm.1, f32[48,64]{1,0:T(8,128)} %lat_hbm.1, ...), custom_call_target="tpu_custom_call" | custom-call | tf_op jit(solution)/shard_map/pallas_call | solution.py:420
  148.1 1.0 shard_map.95
